TPU v7x, 512 devices: a whole 4x4x16 slice. The times are simulated.
512 devices in a mesh: blk: 128 (over y, x, z_lo, core), inner: 4 (over z_hi).
Axes of the slice: x: 4, y: 4, z: 16 (z_hi: 4, z_lo: 4; z = z_hi * 4 + z_lo), core: 2. Of those that a mesh axis runs over, the one named last changes fastest.
Arguments:
- query_latent: bfloat16 [16384, 16384], P('blk', 'inner'), may hold values from -100 to 100
- query_rotary: bfloat16 [16384, 2048], P('blk', 'inner'), may hold values from -100 to 100
- upstream: bfloat16 [16384, 16384], P('blk', 'inner'), may hold values from -6 to 6
- latent: bfloat16 [16384, 512], P(('blk', 'inner')), may hold values from -8 to 8
- key_rotary: bfloat16 [16384, 64], P(('blk', 'inner')), may hold values from -8 to 8
- pattern: int32 [128, 6], P('blk'), may hold values from -1 to 127, as said below
Outputs:
- query_cotangent: bfloat16 [16384, 16384], P('blk', 'inner')
- rotary_cotangent: bfloat16 [16384, 2048], P('blk', 'inner')
- latent_cotangent: float32 [16384, 512], P(('blk', 'inner'))
- positional_cotangent: float32 [16384, 64], P(('blk', 'inner'))
Inputs may be any that keep to these rules, and one draw needn't show every extreme that they name: `pattern`: let d_0 < d_1 < ... be the distinct numbers among 0 to 1 and m * 16 for m = 1 to 4; there are 6 of them. Entry k of row q is either q - d_k or -1, and it is -1 whenever q - d_k < 0. Entry 0 of every row is q.
All inputs are finite; a program needn't handle non-finite values.
Results may differ from a plain program's by a relative error of at most 0.0085.
Values may be sent and summed in bfloat16 or wider, within the bound.
A program may use at most 128 MiB of HBM per device.

v0:
```python
import jax
import jax.numpy as jnp
from jax import lax
from jax.sharding import PartitionSpec as P

LATENT = 512
ROPE = 64
NOPE = 128
WIN = 2
NSTR = 4


def passed_along(value, axis, steps):
    count = lax.axis_size(axis)
    first, last = (max(0, -steps), min(count, count - steps))
    return lax.ppermute(value, axis, [(source, source + steps) for source in range(first, last)])


def sent_together(arrays, axis, dim, along):
    widths = [a.shape[along] for a in arrays]
    both = jnp.concatenate(arrays, axis=along)
    out = lax.all_gather(both, axis, axis=dim, tiled=True)
    return tuple(jnp.split(out, [sum(widths[:k]) for k in range(1, len(widths))], axis=along))


def in_blocks(x, dim, size):
    before, after = (x.shape[:dim], x.shape[dim + 1 :])
    return jnp.moveaxis(x.reshape(*before, size, -1, *after), dim, 0)


def sent_and_summed(x, axis, dim):
    size = lax.axis_size(axis)
    parts = lax.all_to_all(in_blocks(x, dim, size), axis, 0, 0, tiled=True)
    return jnp.sum(parts, axis=0)


def spacing_list(blocks):
    spacing = blocks // 8
    listed = set(range(WIN))
    for number in range(1, NSTR + 1):
        listed.add(number * spacing)
    return sorted(listed)


def fetch_block(full_block, distance):
    if distance == 0:
        return full_block
    return passed_along((full_block[0], full_block[1]), "blk", distance)


def block_scores(
    query_rows, rotary_rows, upstream_rows, key_block, rope_block, causal, softmax_scale, diagonal
):
    scores = (
        jnp.einsum("rl,sl->rs", query_rows, key_block, preferred_element_type=jnp.float32)
        + jnp.einsum("rl,sl->rs", rotary_rows, rope_block, preferred_element_type=jnp.float32)
    ) * softmax_scale
    if diagonal:
        scores = jnp.where(causal, scores, -jnp.inf)
    dprobs = jnp.einsum("rl,sl->rs", upstream_rows, key_block, preferred_element_type=jnp.float32)
    return (scores, dprobs)


def split_pair(values):
    upper = values.astype(jnp.bfloat16)
    lower = (values - upper.astype(jnp.float32)).astype(jnp.bfloat16)
    return (upper, lower)


def paired_product(form, pair, other):
    return jnp.einsum(form, pair[0], other, preferred_element_type=jnp.float32) + jnp.einsum(
        form, pair[1], other, preferred_element_type=jnp.float32
    )


def per_device(query_latent, query_rotary, upstream, latent, key_rotary, pattern):
    spacing = spacing_list(lax.axis_size("blk"))
    softmax_scale = (NOPE + ROPE) ** (-0.5)
    tokens = query_latent.shape[0]
    local_heads = query_latent.shape[1] // LATENT
    row_count = tokens * local_heads
    query_rows = query_latent.reshape(row_count, LATENT)
    rotary_rows = query_rotary.reshape(row_count, ROPE)
    upstream_rows = upstream.reshape(row_count, LATENT)
    row_token = lax.broadcasted_iota(jnp.int32, (row_count, tokens), 0) // local_heads
    key_token = lax.broadcasted_iota(jnp.int32, (row_count, tokens), 1)
    causal = key_token <= row_token
    selected = pattern[0] >= 0
    full_block = sent_together((latent, key_rotary), "inner", 0, 1)
    running_state = (
        jnp.full((row_count,), -jnp.inf, jnp.float32),
        jnp.zeros((row_count,), jnp.float32),
        jnp.zeros((row_count,), jnp.float32),
    )
    stored = []
    kept_scores = []
    for ordinal, distance in enumerate(spacing):
        key_block, rope_block = fetch_block(full_block, distance)
        stored.append((key_block, rope_block))

        def update(
            running_state, key_block=key_block, rope_block=rope_block, diagonal=distance == 0
        ):
            running, denominator, weighted = running_state
            scores, dprobs = block_scores(
                query_rows,
                rotary_rows,
                upstream_rows,
                key_block,
                rope_block,
                causal,
                softmax_scale,
                diagonal,
            )
            newmax = jnp.maximum(running, jnp.max(scores, axis=1))
            factor = jnp.exp(running - newmax)
            exponent = jnp.exp(scores - newmax[:, None])
            return (
                (
                    newmax,
                    denominator * factor + jnp.sum(exponent, axis=1),
                    weighted * factor + jnp.sum(exponent * dprobs, axis=1),
                ),
                scores,
                dprobs,
            )

        def passthrough(running_state):
            return (
                running_state,
                jnp.zeros((row_count, tokens), jnp.float32),
                jnp.zeros((row_count, tokens), jnp.float32),
            )

        running_state, scores, dprobs = lax.cond(
            selected[ordinal], update, passthrough, running_state
        )
        kept_scores.append((scores, dprobs))
    running, denominator, weighted = running_state
    log_total = running + jnp.log(denominator)
    correction = weighted / denominator
    query_sum = jnp.zeros((row_count, LATENT), jnp.float32)
    rotary_sum = jnp.zeros((row_count, ROPE), jnp.float32)
    latent_sum = jnp.zeros((tokens, LATENT), jnp.float32)
    positional_sum = jnp.zeros((tokens, ROPE), jnp.float32)
    for ordinal, distance in enumerate(spacing):
        key_block, rope_block = fetch_block(full_block, distance)

        def backward(operand, key_block=key_block, rope_block=rope_block):
            scores, dprobs = operand
            weights = jnp.exp(scores - log_total[:, None])
            dscores = weights * (dprobs - correction[:, None])
            score_pair = split_pair(dscores)
            weight_pair = split_pair(weights)
            part_query = paired_product("rs,sl->rl", score_pair, key_block)
            part_rotary = paired_product("rs,sl->rl", score_pair, rope_block)
            key_part = softmax_scale * paired_product(
                "rs,rl->sl", score_pair, query_rows
            ) + paired_product("rs,rl->sl", weight_pair, upstream_rows)
            rope_part = softmax_scale * paired_product("rs,rl->sl", score_pair, rotary_rows)
            return (part_query, part_rotary, key_part, rope_part)

        def skipped(operand):
            return (
                jnp.zeros((row_count, LATENT), jnp.float32),
                jnp.zeros((row_count, ROPE), jnp.float32),
                jnp.zeros((tokens, LATENT), jnp.float32),
                jnp.zeros((tokens, ROPE), jnp.float32),
            )

        part_query, part_rotary, key_part, rope_part = lax.cond(
            selected[ordinal], backward, skipped, kept_scores[ordinal]
        )
        query_sum = query_sum + part_query
        rotary_sum = rotary_sum + part_rotary
        if distance > 0:
            key_part, rope_part = passed_along((key_part, rope_part), "blk", -distance)
        latent_sum = latent_sum + key_part
        positional_sum = positional_sum + rope_part
    latent_sum, positional_sum = (
        sent_and_summed(latent_sum, "inner", 0),
        sent_and_summed(positional_sum, "inner", 0),
    )
    query_cotangent = (
        (softmax_scale * query_sum).astype(jnp.bfloat16).reshape(tokens, local_heads * LATENT)
    )
    rotary_cotangent = (
        (softmax_scale * rotary_sum).astype(jnp.bfloat16).reshape(tokens, local_heads * ROPE)
    )
    return (query_cotangent, rotary_cotangent, latent_sum, positional_sum)


def solution(mesh):
    in_specs = (
        P("blk", "inner"),
        P("blk", "inner"),
        P("blk", "inner"),
        P(("blk", "inner"), None),
        P(("blk", "inner"), None),
        P("blk", None),
    )
    out_specs = (
        P("blk", "inner"),
        P("blk", "inner"),
        P(("blk", "inner"), None),
        P(("blk", "inner"), None),
    )
    return jax.shard_map(
        per_device, mesh=mesh, in_specs=in_specs, out_specs=out_specs, check_vma=False
    )
```

profile of v0, /device:TPU:94, one launch (start us, length us, event | category | flops | bytes accessed | tf_op | source)
XLA Modules:
  0.0 234.0 jit_solution(2375425405232842815)
XLA Ops:
  1.5 24.1 %all_gather.3 = bf16[128,576]{1,0:T(8,128)(2,1)S(1)} all-gather(bf16[32,576]{1,0:T(8,128)(2,1)S(1)} %pad_maximum_fusion), channel_id=1, replica_groups=mesh['blk'=128,'inner'=4] {'inner'}, dimensions={0}, use_global_device_ids=true | all-gather | bytes 184320 | tf_op jit(solution)/shard_map/all_gather | solution.py:22
  30.7 3.0 %collective-permute-start = (bf16[128,512]{1,0:T(8,128)(2,1)S(1)}, bf16[128,512]{1,0:T(8,128)(2,1)S(1)}, u32[]{:S(2)}, u32[]{:S(2)}) collective-permute-start(bf16[128,512]{1,0:T(8,128)(2,1)S(1)} %split.8), channel_id=1, source_target_pairs={{0,4},{4,8},{8,12},{12,16},{16,20},{20,24},{24,28},{28,32},{32,36}... | collective-permute-start | bytes 393224 | tf_op jit(solution)/shard_map/ppermute | solution.py:16
  41.0 2.5 %collective-permute-done.2 = bf16[128,512]{1,0:T(8,128)(2,1)S(1)} collective-permute-done((bf16[128,512]{1,0:T(8,128)(2,1)S(1)}, bf16[128,512]{1,0:T(8,128)(2,1)S(1)}, u32[]{:S(2)}, u32[]{:S(2)}) %collective-permute-start.2) | collective-permute-done | bytes 131104 | tf_op jit(solution)/shard_map/ppermute | solution.py:16
  52.7 5.2 %conditional.12 = (f32[1024]{0:T(1024)}, f32[1024]{0:T(1024)S(1)}, f32[1024]{0:T(1024)S(1)}, f32[1024,128]{0,1:T(8,128)}, f32[1024,128]{0,1:T(8,128)S(1)}) conditional(s32[]{:T(128)} %bitcast, () %tuple.118, (s32[1024]{0:T(1024)S(1)}, s32[1024,128]{0,1:T(8,128)S(1)}, bf16[1024,512]{1,0:T(8,128)(2,1)S(1)}, bf16[128,512]{1,0:T(8,128)(2,1)S(1)}, ...), branch_computations={%region_0.1_spmd, %region_1.5_spmd} | conditional | flops 286531584 | bytes 5716008 | solution.py:135
  58.7 5.0 %conditional.13 = (f32[1024]{0:T(1024)}, f32[1024]{0:T(1024)S(1)}, f32[1024]{0:T(1024)S(1)}, f32[1024,128]{0,1:T(8,128)}, f32[1024,128]{0,1:T(8,128)S(1)}) conditional(s32[]{:T(128)} %bitcast.5, (f32[1024]{0:T(1024)}, f32[1024]{0:T(1024)S(1)}, f32[1024]{0:T(1024)S(1)}) %tuple.120, (bf16[1024,512]{1,0:T(8,128)(2,1)S(1)}, ...), branch_computations={%region_5.6_spmd, %region_6.10_spmd} | conditional | flops 286133248 | bytes 5197864 | solution.py:135
  66.2 5.0 %conditional.15 = (f32[1024]{0:T(1024)}, f32[1024]{0:T(1024)S(1)}, f32[1024]{0:T(1024)S(1)}, f32[1024,128]{0,1:T(8,128)}, f32[1024,128]{0,1:T(8,128)S(1)}) conditional(s32[]{:T(128)} %bitcast.3, (f32[1024]{0:T(1024)}, f32[1024]{0:T(1024)S(1)}, f32[1024]{0:T(1024)S(1)}) %tuple.124, (bf16[1024,512]{1,0:T(8,128)(2,1)S(1)}, ...), branch_computations={%region_15.16_spmd, %region_16.20_spmd} | conditional | flops 286133248 | bytes 5197864 | solution.py:135
  73.8 5.8 %conditional.17 = (f32[1024]{0:T(1024)}, f32[1024]{0:T(1024)S(1)}, f32[1024]{0:T(1024)S(1)}, f32[1024,128]{0,1:T(8,128)}, f32[1024,128]{0,1:T(8,128)}) conditional(s32[]{:T(128)} %bitcast.1, (f32[1024]{0:T(1024)}, f32[1024]{0:T(1024)S(1)}, f32[1024]{0:T(1024)S(1)}) %tuple.128, (bf16[1024,512]{1,0:T(8,128)(2,1)S(1)}, ...), branch_computations={%region_25.26_spmd, %region_26.30_spmd} | conditional | flops 286133248 | bytes 5197864 | solution.py:135
  76.0 2.3 multiply_reduce_fusion.5
  80.3 12.8 %conditional.23 = (f32[1024,512]{1,0:T(8,128)}, f32[1024,64]{0,1:T(8,128)}, f32[128,512]{1,0:T(8,128)}, f32[128,64]{0,1:T(8,128)}) conditional(s32[]{:T(128)} %bitcast.1, () %tuple.139, (f32[1024]{0:T(1024)S(1)}, f32[1024,128]{0,1:T(8,128)}, f32[1024]{0:T(1024)S(1)}, f32[1024,128]{0,1:T(8,128)}, bf16[128,512]{1,0:T(8,128)(2,1)S(1)}, ...), branch_computations={%region_40.41_spmd, %region_41.42_spmd} | conditional | flops 875118592 | bytes 21774480 | solution.py:171
  96.5 3.6 %conditional.22 = (f32[1024,512]{1,0:T(8,128)}, f32[1024,64]{0,1:T(8,128)}, f32[128,512]{1,0:T(8,128)}, f32[128,64]{0,1:T(8,128)}) conditional(s32[]{:T(128)} %bitcast.2, () %tuple.137, (f32[1024]{0:T(1024)S(1)}, f32[1024,128]{0,1:T(8,128)}, f32[1024]{0:T(1024)S(1)}, f32[1024,128]{0,1:T(8,128)}, bf16[128,512]{1,0:T(8,128)(2,1)S(1)}, ...), branch_computations={%region_38.39_spmd, %region_39.40_spmd} | conditional | flops 875118592 | bytes 20594720 | solution.py:171
  101.6 23.8 %collective-permute-start.18 = (f32[128,64]{1,0:T(8,128)}, f32[128,64]{1,0:T(8,128)}, u32[]{:S(2)}, u32[]{:S(2)}) collective-permute-start(f32[128,64]{1,0:T(8,128)} %copy.40), channel_id=1, source_target_pairs={{192,0},{196,4},{200,8},{204,12},{208,16},{212,20},{216,24},{220,2... | collective-permute-start | bytes 98312 | tf_op jit(solution)/shard_map/ppermute | solution.py:16
  125.4 11.1 %conditional.21 = (f32[1024,512]{1,0:T(8,128)}, f32[1024,64]{0,1:T(8,128)}, f32[128,512]{1,0:T(8,128)}, f32[128,64]{0,1:T(8,128)S(1)}) conditional(s32[]{:T(128)} %bitcast.3, () %tuple.135, (f32[1024]{0:T(1024)S(1)}, f32[1024,128]{0,1:T(8,128)}, f32[1024]{0:T(1024)S(1)}, f32[1024,128]{0,1:T(8,128)}, bf16[128,512]{1,0:T(8,128)(2,1)S(1)}, ...), branch_computations={%region_36.37_spmd, %region_37.38_spmd} | conditional | flops 875118592 | bytes 20660284 | solution.py:171
  139.2 3.7 %conditional.20 = (f32[1024,512]{1,0:T(8,128)}, f32[1024,64]{0,1:T(8,128)}, f32[128,512]{1,0:T(8,128)}, f32[128,64]{0,1:T(8,128)}) conditional(s32[]{:T(128)} %bitcast.4, () %tuple.133, (f32[1024]{0:T(1024)S(1)}, f32[1024,128]{0,1:T(8,128)}, f32[1024]{0:T(1024)S(1)}, f32[1024,128]{0,1:T(8,128)}, bf16[128,512]{1,0:T(8,128)(2,1)S(1)}, ...), branch_computations={%region_34.35_spmd, %region_35.36_spmd} | conditional | flops 875118592 | bytes 20660284 | solution.py:171
  144.3 10.5 %collective-permute-start.16 = (f32[128,64]{1,0:T(8,128)}, f32[128,64]{1,0:T(8,128)S(1)}, u32[]{:S(2)}, u32[]{:S(2)}) collective-permute-start(f32[128,64]{1,0:T(8,128)} %copy.38), channel_id=1, source_target_pairs={{64,0},{68,4},{72,8},{76,12},{80,16},{84,20},{88,24},{92,28},{96,3... | collective-permute-start | bytes 98312 | tf_op jit(solution)/shard_map/ppermute | solution.py:16
  154.9 11.2 %conditional.19 = (f32[1024,512]{1,0:T(8,128)}, f32[1024,64]{0,1:T(8,128)}, f32[128,512]{1,0:T(8,128)}, f32[128,64]{0,1:T(8,128)S(1)}) conditional(s32[]{:T(128)} %bitcast.5, () %tuple.131, (f32[1024]{0:T(1024)S(1)}, f32[1024,128]{0,1:T(8,128)}, f32[1024]{0:T(1024)S(1)}, f32[1024,128]{0,1:T(8,128)}, bf16[128,512]{1,0:T(8,128)(2,1)S(1)}, ...), branch_computations={%region_32.33_spmd, %region_33.34_spmd} | conditional | flops 875118592 | bytes 20660284 | solution.py:171
  170.2 2.2 collective-permute-start.13
  174.4 2.6 %collective-permute-start.11 = (f32[128,512]{1,0:T(8,128)}, f32[128,512]{1,0:T(8,128)}, u32[]{:S(2)}, u32[]{:S(2)}) collective-permute-start(f32[128,512]{1,0:T(8,128)} %get-tuple-element.517), channel_id=1, source_target_pairs={{64,0},{68,4},{72,8},{76,12},{80,16},{84,20},{88,24},{92,28},{96,3... | collective-permute-start | bytes 786440 | tf_op jit(solution)/shard_map/ppermute | solution.py:16
  178.9 12.8 %conditional.18 = (f32[1024,512]{1,0:T(8,128)}, f32[1024,64]{0,1:T(8,128)}, f32[128,512]{1,0:T(8,128)}, f32[128,64]{1,0:T(8,128)S(1)}) conditional(s32[]{:T(128)} %bitcast, () %tuple.117, (f32[1024]{0:T(1024)S(1)}, f32[1024,128]{0,1:T(8,128)}, f32[1024]{0:T(1024)S(1)}, f32[1024,128]{0,1:T(8,128)}, bf16[128,512]{1,0:T(8,128)(2,1)S(1)}, ...), branch_computations={%region_30.31_spmd, %region_31.32_spmd} | conditional | flops 875118592 | bytes 20660256 | solution.py:171
  193.4 6.6 %all-to-all-start.1 = ((f32[4,1,2048]{2,1,0:T(1,128)}), f32[4,1,2048]{2,1,0:T(1,128)S(1)}, u32[]{:S(2)}, u32[]{:S(2)}) async-start(f32[4,1,2048]{2,1,0:T(1,128)} %reshape.92), calls=%async_computation.1 | async-start | bytes 65536 | tf_op jit(solution)/shard_map/all_to_all | solution.py:33
  200.0 2.2 add_add_fusion
  202.2 10.5 %all-to-all-done.1 = f32[4,1,2048]{2,1,0:T(1,128)S(1)} async-done(((f32[4,1,2048]{2,1,0:T(1,128)}), f32[4,1,2048]{2,1,0:T(1,128)S(1)}, u32[]{:S(2)}, u32[]{:S(2)}) %all-to-all-start.1) | async-done | bytes 32800 | tf_op jit(solution)/shard_map/all_to_all | solution.py:33
  212.7 3.4 %all-to-all-start = ((f32[4,32,512]{2,1,0:T(8,128)}), f32[4,32,512]{2,1,0:T(8,128)S(1)}, u32[]{:S(2)}, u32[]{:S(2)}) async-start(f32[4,32,512]{2,1,0:T(8,128)} %bitcast.6), calls=%async_computation | async-start | bytes 524288 | tf_op jit(solution)/shard_map/all_to_all | solution.py:33
  216.1 6.1 %multiply_convert_fusion = bf16[1024,512]{1,0:T(8,128)(2,1)S(1)} fusion(f32[1024,512]{1,0:T(8,128)} %get-tuple-element.508, f32[1024,512]{1,0:T(8,128)} %get-tuple-element.505, f32[1024,512]{1,0:T(8,128)} %get-tuple-element.502, f32[1024,512]{1,0:T(8,128)} %get-tuple-element.499, f32[1024,512]{1,0:T(8,128)} %get-tuple-element.493, ...), kind=kLoop, calls=%fused_computation.157 | loop fusion | flops 3670016 | bytes 13631488 | tf_op jit(solution)/shard_map/convert_element_type | solution.py:185
  228.1 5.3 %all-to-all-done = f32[4,32,512]{2,1,0:T(8,128)S(1)} async-done(((f32[4,32,512]{2,1,0:T(8,128)}), f32[4,32,512]{2,1,0:T(8,128)S(1)}, u32[]{:S(2)}, u32[]{:S(2)}) %all-to-all-start) | async-done | bytes 262176 | tf_op jit(solution)/shard_map/all_to_all | solution.py:33
  (181 shorter events, 125.2 us)
Async XLA Ops:
  0.6 50.2 %copy-start.15 = (bf16[128,512]{1,0:T(8,128)(2,1)S(1)}, bf16[128,512]{1,0:T(8,128)(2,1)}, u32[]{:S(2)}) copy-start(bf16[128,512]{1,0:T(8,128)(2,1)} %param.31) | copy-start | bytes 393220
  26.2 8.9 %collective-permute-start.1 = (bf16[128,64]{1,0:T(8,128)(2,1)}, bf16[128,64]{1,0:T(8,128)(2,1)S(1)}, u32[]{:S(2)}, u32[]{:S(2)}) collective-permute-start(bf16[128,64]{1,0:T(8,128)(2,1)} %split.9), channel_id=1, source_target_pairs={{0,4},{4,8},{8,12},{12,16},{16,20},{20,24},{24,28},{28,32},{32,36}... | collective-permute-start | bytes 49160 | tf_op jit(solution)/shard_map/ppermute | solution.py:16
  28.1 8.3 %collective-permute-start.3 = (bf16[128,64]{1,0:T(8,128)(2,1)}, bf16[128,64]{1,0:T(8,128)(2,1)S(1)}, u32[]{:S(2)}, u32[]{:S(2)}) collective-permute-start(bf16[128,64]{1,0:T(8,128)(2,1)} %split.9), channel_id=1, source_target_pairs={{0,64},{4,68},{8,72},{12,76},{16,80},{20,84},{24,88},{28,92},{32,9... | collective-permute-start | bytes 49160 | tf_op jit(solution)/shard_map/ppermute | solution.py:16
  29.4 8.3 %collective-permute-start.5 = (bf16[128,64]{1,0:T(8,128)(2,1)}, bf16[128,64]{1,0:T(8,128)(2,1)S(1)}, u32[]{:S(2)}, u32[]{:S(2)}) collective-permute-start(bf16[128,64]{1,0:T(8,128)(2,1)} %split.9), channel_id=1, source_target_pairs={{0,128},{4,132},{8,136},{12,140},{16,144},{20,148},{24,152},{28,15... | collective-permute-start | bytes 49160 | tf_op jit(solution)/shard_map/ppermute | solution.py:16
  30.7 9.0 %collective-permute-start = (bf16[128,512]{1,0:T(8,128)(2,1)S(1)}, bf16[128,512]{1,0:T(8,128)(2,1)S(1)}, u32[]{:S(2)}, u32[]{:S(2)}) collective-permute-start(bf16[128,512]{1,0:T(8,128)(2,1)S(1)} %split.8), channel_id=1, source_target_pairs={{0,4},{4,8},{8,12},{12,16},{16,20},{20,24},{24,28},{28,32},{32,36}... | collective-permute-start | bytes 393224 | tf_op jit(solution)/shard_map/ppermute | solution.py:16
  33.8 9.7 %collective-permute-start.2 = (bf16[128,512]{1,0:T(8,128)(2,1)S(1)}, bf16[128,512]{1,0:T(8,128)(2,1)S(1)}, u32[]{:S(2)}, u32[]{:S(2)}) collective-permute-start(bf16[128,512]{1,0:T(8,128)(2,1)S(1)} %split.8), channel_id=1, source_target_pairs={{0,64},{4,68},{8,72},{12,76},{16,80},{20,84},{24,88},{28,92},{32,9... | collective-permute-start | bytes 393224 | tf_op jit(solution)/shard_map/ppermute | solution.py:16
  35.1 30.3 %collective-permute-start.4 = (bf16[128,512]{1,0:T(8,128)(2,1)S(1)}, bf16[128,512]{1,0:T(8,128)(2,1)S(1)}, u32[]{:S(2)}, u32[]{:S(2)}) collective-permute-start(bf16[128,512]{1,0:T(8,128)(2,1)S(1)} %split.8), channel_id=1, source_target_pairs={{0,128},{4,132},{8,136},{12,140},{16,144},{20,148},{24,152},{28,15... | collective-permute-start | bytes 393224 | tf_op jit(solution)/shard_map/ppermute | solution.py:16
  36.4 34.9 %collective-permute-start.6 = (bf16[128,512]{1,0:T(8,128)(2,1)S(1)}, bf16[128,512]{1,0:T(8,128)(2,1)S(1)}, u32[]{:S(2)}, u32[]{:S(2)}) collective-permute-start(bf16[128,512]{1,0:T(8,128)(2,1)S(1)} %split.8), channel_id=1, source_target_pairs={{0,192},{4,196},{8,200},{12,204},{16,208},{20,212},{24,216},{28,22... | collective-permute-start | bytes 393224 | tf_op jit(solution)/shard_map/ppermute | solution.py:16
  37.7 27.7 %copy-start.11 = (bf16[128,64]{1,0:T(8,128)(2,1)}, bf16[128,64]{1,0:T(8,128)(2,1)S(1)}, u32[]{:S(2)}) copy-start(bf16[128,64]{1,0:T(8,128)(2,1)S(1)} %collective-permute-done.5) | copy-start | bytes 49156
  37.7 35.2 %collective-permute-start.8 = (bf16[128,512]{1,0:T(8,128)(2,1)S(1)}, bf16[128,512]{1,0:T(8,128)(2,1)S(1)}, u32[]{:S(2)}, u32[]{:S(2)}) collective-permute-start(bf16[128,512]{1,0:T(8,128)(2,1)S(1)} %split.8), channel_id=1, source_target_pairs={{0,256},{4,260},{8,264},{12,268},{16,272},{20,276},{24,280},{28,28... | collective-permute-start | bytes 393224 | tf_op jit(solution)/shard_map/ppermute | solution.py:16
  39.7 31.6 %collective-permute-start.7 = (bf16[128,64]{1,0:T(8,128)(2,1)}, bf16[128,64]{1,0:T(8,128)(2,1)}, u32[]{:S(2)}, u32[]{:S(2)}) collective-permute-start(bf16[128,64]{1,0:T(8,128)(2,1)} %split.9), channel_id=1, source_target_pairs={{0,192},{4,196},{8,200},{12,204},{16,208},{20,212},{24,216},{28,22... | collective-permute-start | bytes 49160 | tf_op jit(solution)/shard_map/ppermute | solution.py:16
  43.5 29.5 %collective-permute-start.9 = (bf16[128,64]{1,0:T(8,128)(2,1)}, bf16[128,64]{1,0:T(8,128)(2,1)S(1)}, u32[]{:S(2)}, u32[]{:S(2)}) collective-permute-start(bf16[128,64]{1,0:T(8,128)(2,1)} %split.9), channel_id=1, source_target_pairs={{0,256},{4,260},{8,264},{12,268},{16,272},{20,276},{24,280},{28,28... | collective-permute-start | bytes 49160 | tf_op jit(solution)/shard_map/ppermute | solution.py:16
  94.6 73.6 %collective-permute-start.19 = (f32[128,64]{1,0:T(8,128)}, f32[128,64]{1,0:T(8,128)}, u32[]{:S(2)}, u32[]{:S(2)}) collective-permute-start(f32[128,64]{1,0:T(8,128)} %copy.41), channel_id=1, source_target_pairs={{256,0},{260,4},{264,8},{268,12},{272,16},{276,20},{280,24},{284,2... | collective-permute-start | bytes 98312 | tf_op jit(solution)/shard_map/ppermute | solution.py:16
  101.6 68.6 %collective-permute-start.18 = (f32[128,64]{1,0:T(8,128)}, f32[128,64]{1,0:T(8,128)}, u32[]{:S(2)}, u32[]{:S(2)}) collective-permute-start(f32[128,64]{1,0:T(8,128)} %copy.40), channel_id=1, source_target_pairs={{192,0},{196,4},{200,8},{204,12},{208,16},{212,20},{216,24},{220,2... | collective-permute-start | bytes 98312 | tf_op jit(solution)/shard_map/ppermute | solution.py:16
  137.2 35.1 %collective-permute-start.17 = (f32[128,64]{1,0:T(8,128)}, f32[128,64]{1,0:T(8,128)}, u32[]{:S(2)}, u32[]{:S(2)}) collective-permute-start(f32[128,64]{1,0:T(8,128)} %copy.39), channel_id=1, source_target_pairs={{128,0},{132,4},{136,8},{140,12},{144,16},{148,20},{152,24},{156,2... | collective-permute-start | bytes 98312 | tf_op jit(solution)/shard_map/ppermute | solution.py:16
  144.3 30.0 %collective-permute-start.16 = (f32[128,64]{1,0:T(8,128)}, f32[128,64]{1,0:T(8,128)S(1)}, u32[]{:S(2)}, u32[]{:S(2)}) collective-permute-start(f32[128,64]{1,0:T(8,128)} %copy.38), channel_id=1, source_target_pairs={{64,0},{68,4},{72,8},{76,12},{80,16},{84,20},{88,24},{92,28},{96,3... | collective-permute-start | bytes 98312 | tf_op jit(solution)/shard_map/ppermute | solution.py:16
  166.2 10.8 %collective-permute-start.15 = (f32[128,64]{1,0:T(8,128)S(1)}, f32[128,64]{1,0:T(8,128)S(1)}, u32[]{:S(2)}, u32[]{:S(2)}) collective-permute-start(f32[128,64]{1,0:T(8,128)S(1)} %copy.36), channel_id=1, source_target_pairs={{4,0},{8,4},{12,8},{16,12},{20,16},{24,20},{28,24},{32,28},{36,32}... | collective-permute-start | bytes 98312 | tf_op jit(solution)/shard_map/ppermute | solution.py:16
  168.2 31.8 %collective-permute-start.14 = (f32[128,512]{1,0:T(8,128)}, f32[128,512]{1,0:T(8,128)}, u32[]{:S(2)}, u32[]{:S(2)}) collective-permute-start(f32[128,512]{1,0:T(8,128)} %get-tuple-element.520), channel_id=1, source_target_pairs={{256,0},{260,4},{264,8},{268,12},{272,16},{276,20},{280,24},{284,2... | collective-permute-start | bytes 786440 | tf_op jit(solution)/shard_map/ppermute | solution.py:16
  170.2 29.8 %collective-permute-start.13 = (f32[128,512]{1,0:T(8,128)}, f32[128,512]{1,0:T(8,128)}, u32[]{:S(2)}, u32[]{:S(2)}) collective-permute-start(f32[128,512]{1,0:T(8,128)} %get-tuple-element.519), channel_id=1, source_target_pairs={{192,0},{196,4},{200,8},{204,12},{208,16},{212,20},{216,24},{220,2... | collective-permute-start | bytes 786440 | tf_op jit(solution)/shard_map/ppermute | solution.py:16
  172.4 27.6 %collective-permute-start.12 = (f32[128,512]{1,0:T(8,128)}, f32[128,512]{1,0:T(8,128)}, u32[]{:S(2)}, u32[]{:S(2)}) collective-permute-start(f32[128,512]{1,0:T(8,128)} %get-tuple-element.518), channel_id=1, source_target_pairs={{128,0},{132,4},{136,8},{140,12},{144,16},{148,20},{152,24},{156,2... | collective-permute-start | bytes 786440 | tf_op jit(solution)/shard_map/ppermute | solution.py:16
  174.4 25.6 %collective-permute-start.11 = (f32[128,512]{1,0:T(8,128)}, f32[128,512]{1,0:T(8,128)}, u32[]{:S(2)}, u32[]{:S(2)}) collective-permute-start(f32[128,512]{1,0:T(8,128)} %get-tuple-element.517), channel_id=1, source_target_pairs={{64,0},{68,4},{72,8},{76,12},{80,16},{84,20},{88,24},{92,28},{96,3... | collective-permute-start | bytes 786440 | tf_op jit(solution)/shard_map/ppermute | solution.py:16
  177.0 23.0 %collective-permute-start.10 = (f32[128,512]{1,0:T(8,128)}, f32[128,512]{1,0:T(8,128)}, u32[]{:S(2)}, u32[]{:S(2)}) collective-permute-start(f32[128,512]{1,0:T(8,128)} %get-tuple-element.516), channel_id=1, source_target_pairs={{4,0},{8,4},{12,8},{16,12},{20,16},{24,20},{28,24},{32,28},{36,32}... | collective-permute-start | bytes 786440 | tf_op jit(solution)/shard_map/ppermute | solution.py:16
  193.4 19.4 %all-to-all-start.1 = ((f32[4,1,2048]{2,1,0:T(1,128)}), f32[4,1,2048]{2,1,0:T(1,128)S(1)}, u32[]{:S(2)}, u32[]{:S(2)}) async-start(f32[4,1,2048]{2,1,0:T(1,128)} %reshape.92), calls=%async_computation.1 | async-start | bytes 65536 | tf_op jit(solution)/shard_map/all_to_all | solution.py:33
  212.7 20.6 %all-to-all-start = ((f32[4,32,512]{2,1,0:T(8,128)}), f32[4,32,512]{2,1,0:T(8,128)S(1)}, u32[]{:S(2)}, u32[]{:S(2)}) async-start(f32[4,32,512]{2,1,0:T(8,128)} %bitcast.6), calls=%async_computation | async-start | bytes 524288 | tf_op jit(solution)/shard_map/all_to_all | solution.py:33
  (13 other events, 66.5 us)
where the time goes:
time: 237 us; the launch traced here: 234 us
  starting transfers between devices  76 us (32%)
  matrix products  43.1 us (18%)
  local copies, waits for them, and re-layouts  41.8 us (18%)
  other arithmetic  25.3 us (11%)
  blocking collectives  24.1 us (10%)
  waiting for transfers between devices  18.3 us (8%)
  between operations  4.87 us (2%)
    ppermute x20, starting transfers between devices, passed_along(): lax.ppermute(value, axis, [(source, source + steps) for source in range(f...  66 us
    all_gather x1, blocking collectives, sent_together(): out = lax.all_gather(both, axis, axis=dim, tiled=True)  24.1 us
    another operation x20, local copies, waits for them, and re-layouts  22.3 us
    dot_general x20, matrix products, paired_product(): jnp.einsum(form, pair[1], other, preferred_element_type=jnp.float32)  19.9 us
    all_to_all x2, waiting for transfers between devices, sent_and_summed(): parts = lax.all_to_all(in_blocks(x, dim, size), axis, 0, 0, tiled=True)  15.8 us
    all_to_all x2, starting transfers between devices, sent_and_summed(): parts = lax.all_to_all(in_blocks(x, dim, size), axis, 0, 0, tiled=True)  10 us
    dot_general x20, matrix products, paired_product(): jnp.einsum(form, pair[0], other, preferred_element_type=jnp.float32)  8.87 us
    dot_general x4, matrix products, block_scores(): jnp.einsum('rl,sl->rs', upstream_rows, key_block, preferred_element_type=...  6.89 us
  transfers between devices with their start and end apart: 22, of which 3 were waited for; matrix products, arithmetic and copies ran while one was open for 36% of the time, Pallas kernels for 0%

commit v1 on v0

v1 whole, which is shorter than its diff:
```python
import functools

import jax
import jax.numpy as jnp
from jax import lax
from jax.experimental import pallas as pl
from jax.experimental.pallas import tpu as pltpu
from jax.sharding import PartitionSpec as P

MESH = pl.DeviceIdType.MESH
LATENT = 512
ROPE = 64
NOPE = 128
WIN = 2
NSTR = 4
LOG2E = 1.4426950408889634
MASKED = -1e30
SLOT_ORDER = (0, 1, 3, 2)
GRAD_ORDER = (2, 1, 3, 0)


def spacing_list(blocks):
    spacing = blocks // 8
    listed = set(range(WIN))
    for number in range(1, NSTR + 1):
        listed.add(number * spacing)
    return sorted(listed)


def kernel(
    blocks,
    groups,
    spacing,
    scale,
    q_hbm,
    qr_hbm,
    up_hbm,
    lat_ref,
    kr_ref,
    pat_ref,
    qc_ref,
    rc_ref,
    lc_ref,
    pc_ref,
    qcat,
    upcat,
    qrraw,
    kbuf,
    kcat,
    s_buf,
    dp_buf,
    ds_buf,
    w_buf,
    gsend,
    gown,
    gbuf,
    rsend,
    rown,
    rbuf,
    load_sem,
    in_send,
    in_recv,
    k_send,
    k_recv,
    g_send,
    g_recv,
    r_send,
    r_recv,
):
    b = lax.axis_index("blk")
    i = lax.axis_index("inner")
    nd = len(spacing)
    heads = q_hbm.shape[1] // LATENT
    tokens = q_hbm.shape[0]
    rows = heads * tokens
    tile = lat_ref.shape[0]
    half = tile // 2
    per_slot = nd * tile

    def inner_peer(k):
        return (b, lax.rem(i + k, groups))

    def blk_peer(d):
        return (lax.rem(b + d + blocks, blocks), i)

    barrier = pltpu.get_barrier_semaphore()
    partners = {d for d in spacing if d > 0} | {(-d) % blocks for d in spacing if d > 0}
    partners = sorted(partners)
    for k in range(1, groups):
        pl.semaphore_signal(barrier, inc=1, device_id=inner_peer(k), device_id_type=MESH)
    for d in partners:
        pl.semaphore_signal(barrier, inc=1, device_id=blk_peer(d), device_id_type=MESH)

    loads = [pltpu.make_async_copy(qr_hbm, qrraw, load_sem.at[0])]
    for h in range(heads):
        span = pl.ds(h * LATENT, LATENT)
        own = pl.ds(h * tokens, tokens)
        loads.append(
            pltpu.make_async_copy(q_hbm.at[:, span], qcat.at[own, pl.ds(0, LATENT)], load_sem.at[1 + 2 * h])
        )
        loads.append(pltpu.make_async_copy(up_hbm.at[:, span], upcat.at[own], load_sem.at[2 + 2 * h]))
    for load in loads:
        load.start()

    kbuf[0, 0, :, 0:LATENT] = lat_ref[0:half]
    kbuf[0, 0, :, LATENT : 2 * LATENT] = lat_ref[half:tile]
    kbuf[0, 0, :, 2 * LATENT :] = jnp.concatenate([kr_ref[0:half], kr_ref[half:tile]], axis=1)

    pl.semaphore_wait(barrier, groups - 1 + len(partners))

    sends = []
    for k in (2, 1, 3):
        back = (groups - k) % groups
        copy = pltpu.make_async_remote_copy(
            src_ref=kbuf.at[0, 0],
            dst_ref=kbuf.at[back, 0],
            send_sem=in_send.at[k],
            recv_sem=in_recv.at[back],
            device_id=inner_peer(k),
            device_id_type=MESH,
        )
        copy.start()
        sends.append(copy)

    def forward(k):
        for n in range(1, nd):
            copy = pltpu.make_async_remote_copy(
                src_ref=kbuf.at[k, 0],
                dst_ref=kbuf.at[k, n],
                send_sem=k_send.at[k, n],
                recv_sem=k_recv.at[k, n],
                device_id=blk_peer(spacing[n]),
                device_id_type=MESH,
            )
            copy.start()
            sends.append(copy)

    forward(0)
    for k in SLOT_ORDER[1:]:
        pltpu.make_async_remote_copy(
            src_ref=kbuf.at[0, 0],
            dst_ref=kbuf.at[k, 0],
            send_sem=in_send.at[k],
            recv_sem=in_recv.at[k],
            device_id=inner_peer(k),
            device_id_type=MESH,
        ).wait_recv()
        forward(k)

    for load in loads:
        load.wait()
    lane = lax.broadcasted_iota(jnp.int32, (tokens, 2 * ROPE), 1)
    for h in range(heads):
        pair = qrraw[:, pl.ds((h // 2) * 2 * ROPE, 2 * ROPE)]
        keep = (lane < ROPE) if h % 2 == 0 else (lane >= ROPE)
        qcat[pl.ds(h * tokens, tokens), LATENT:] = jnp.where(keep, pair, jnp.zeros_like(pair))

    bias = [jnp.where(pat_ref[0, n] >= 0, 0.0, MASKED).astype(jnp.float32) for n in range(nd)]
    factor = scale * LOG2E
    lane_half = lax.broadcasted_iota(jnp.int32, (half, 2 * ROPE), 1)
    contract_last = (((1,), (1,)), ((), ()))

    for k in SLOT_ORDER:
        for n in range(1, nd):
            pltpu.make_async_remote_copy(
                src_ref=kbuf.at[k, 0],
                dst_ref=kbuf.at[k, n],
                send_sem=k_send.at[k, n],
                recv_sem=k_recv.at[k, n],
                device_id=blk_peer(spacing[n]),
                device_id_type=MESH,
            ).wait_recv()
        base = k * per_slot
        for n in range(nd):
            start = base + n * tile
            kcat[pl.ds(start, half), 0:LATENT] = kbuf[k, n, :, 0:LATENT]
            kcat[pl.ds(start + half, half), 0:LATENT] = kbuf[k, n, :, LATENT : 2 * LATENT]
            both = kbuf[k, n, :, 2 * LATENT :].astype(jnp.float32)
            turned = pltpu.roll(both, ROPE, 1)
            kcat[pl.ds(start, half), LATENT:] = jnp.where(lane_half < ROPE, both, turned).astype(jnp.bfloat16)
            kcat[pl.ds(start + half, half), LATENT:] = jnp.where(lane_half < ROPE, turned, both).astype(jnp.bfloat16)
        keys = kcat[pl.ds(base, per_slot), :]

        def score_step(p, carry, base=base, keys=keys, k=k):
            span = pl.ds(pl.multiple_of(p * 256, 256), 256)
            s = lax.dot_general(keys, qcat[span, :], contract_last, preferred_element_type=jnp.float32) * factor
            dp = lax.dot_general(
                keys[:, 0:LATENT], upcat[span, :], contract_last, preferred_element_type=jnp.float32
            )
            dp_buf[pl.ds(base, per_slot), span] = dp
            key_token = lax.broadcasted_iota(jnp.int32, (tile, 256), 0) + lax.rem(i + k, groups) * tile
            row_token = lax.rem(lax.broadcasted_iota(jnp.int32, (tile, 256), 1), tokens)
            for n in range(nd):
                part = s[n * tile : (n + 1) * tile]
                if n == 0:
                    part = jnp.where(key_token <= row_token, part, MASKED)
                else:
                    part = part + bias[n]
                s_buf[pl.ds(base + n * tile, tile), span] = part
            return carry

        lax.fori_loop(0, rows // 256, score_step, 0)

    def softmax_step(p, carry):
        span = pl.ds(pl.multiple_of(p * 128, 128), 128)
        top = jnp.max(s_buf[:, span], axis=0, keepdims=True)
        e = jnp.exp2(s_buf[:, span] - top)
        total = jnp.sum(e, axis=0, keepdims=True)
        weighted = jnp.sum(e * dp_buf[:, span], axis=0, keepdims=True)
        inverse = 1.0 / total
        correction = weighted * inverse
        w = e * inverse
        w_buf[:, span] = w.astype(jnp.bfloat16)
        ds_buf[:, span] = (w * ((dp_buf[:, span] - correction) * scale)).astype(jnp.bfloat16)
        return carry

    lax.fori_loop(0, rows // 128, softmax_step, 0)

    natural = (((1,), (0,)), ((), ()))

    def pack_rows(g, n):
        lo = g[n * tile : n * tile + half]
        hi = g[n * tile + half : (n + 1) * tile]
        rlo = lo[:, LATENT:]
        rhi = hi[:, LATENT:]
        rlo = rlo + pltpu.roll(rlo, ROPE, 1)
        rhi = rhi + pltpu.roll(rhi, ROPE, 1)
        return lo[:, 0:LATENT], hi[:, 0:LATENT], jnp.where(lane_half < ROPE, rlo, rhi)

    for k in GRAD_ORDER:
        base = k * per_slot
        dsk = ds_buf[pl.ds(base, per_slot), :]
        wk = w_buf[pl.ds(base, per_slot), :]
        g_lat = lax.dot_general(dsk, qcat[:, 0:LATENT], natural, preferred_element_type=jnp.float32)
        g_lat = g_lat + lax.dot_general(wk, upcat[...], natural, preferred_element_type=jnp.float32)
        g_rot = lax.dot_general(dsk, qcat[:, LATENT:], natural, preferred_element_type=jnp.float32)
        g = jnp.concatenate([g_lat, g_rot], axis=1)
        for n in range(nd):
            lo, hi, rot = pack_rows(g, n)
            if n == 0:
                gown[k, :, 0:LATENT] = lo
                gown[k, :, LATENT : 2 * LATENT] = hi
                gown[k, :, 2 * LATENT :] = rot
            else:
                gsend[k, n, :, 0:LATENT] = lo.astype(jnp.bfloat16)
                gsend[k, n, :, LATENT : 2 * LATENT] = hi.astype(jnp.bfloat16)
                gsend[k, n, :, 2 * LATENT :] = rot.astype(jnp.bfloat16)
        for n in range(1, nd):
            copy = pltpu.make_async_remote_copy(
                src_ref=gsend.at[k, n],
                dst_ref=gbuf.at[k, n],
                send_sem=g_send.at[k, n],
                recv_sem=g_recv.at[k, n],
                device_id=blk_peer(-spacing[n]),
                device_id_type=MESH,
            )
            copy.start()
            sends.append(copy)

    lane_tok = lax.broadcasted_iota(jnp.int32, (tokens, 2 * ROPE), 1)
    for p in range(heads // 2):
        out = []
        for h in (2 * p, 2 * p + 1):
            span = pl.ds(h * tokens, tokens)
            dq = lax.dot_general(
                ds_buf[:, span], kcat[...], (((0,), (0,)), ((), ())), preferred_element_type=jnp.float32
            )
            qc_ref[:, pl.ds(h * LATENT, LATENT)] = dq[:, 0:LATENT].astype(jnp.bfloat16)
            out.append(dq[:, LATENT:])
        rc_ref[:, pl.ds(p * 2 * ROPE, 2 * ROPE)] = jnp.where(lane_tok < ROPE, out[0], out[1]).astype(jnp.bfloat16)

    for k in GRAD_ORDER:
        total = gown[k]
        for n in range(1, nd):
            pltpu.make_async_remote_copy(
                src_ref=gsend.at[k, n],
                dst_ref=gbuf.at[k, n],
                send_sem=g_send.at[k, n],
                recv_sem=g_recv.at[k, n],
                device_id=blk_peer(-spacing[n]),
                device_id_type=MESH,
            ).wait_recv()
            total = total + gbuf[k, n].astype(jnp.float32)
        if k == 0:
            rown[...] = total
        else:
            back = (groups - k) % groups
            rsend[k] = total.astype(jnp.bfloat16)
            copy = pltpu.make_async_remote_copy(
                src_ref=rsend.at[k],
                dst_ref=rbuf.at[back],
                send_sem=r_send.at[k],
                recv_sem=r_recv.at[back],
                device_id=inner_peer(k),
                device_id_type=MESH,
            )
            copy.start()
            sends.append(copy)

    total = rown[...]
    for k in range(1, groups):
        pltpu.make_async_remote_copy(
            src_ref=rsend.at[k],
            dst_ref=rbuf.at[k],
            send_sem=r_send.at[k],
            recv_sem=r_recv.at[k],
            device_id=inner_peer(k),
            device_id_type=MESH,
        ).wait_recv()
        total = total + rbuf[k].astype(jnp.float32)
    lc_ref[0:half, :] = total[:, 0:LATENT]
    lc_ref[half:tile, :] = total[:, LATENT : 2 * LATENT]
    pc_ref[0:half, :] = total[:, 2 * LATENT : 2 * LATENT + ROPE]
    pc_ref[half:tile, :] = total[:, 2 * LATENT + ROPE :]
    for copy in sends:
        copy.wait_send()


def per_device(query_latent, query_rotary, upstream, latent, key_rotary, pattern):
    blocks = lax.axis_size("blk")
    groups = lax.axis_size("inner")
    spacing = spacing_list(blocks)
    nd = len(spacing)
    scale = (NOPE + ROPE) ** (-0.5)
    tokens, width = query_latent.shape
    heads = width // LATENT
    rows = heads * tokens
    tile = latent.shape[0]
    half = tile // 2
    packed = 2 * (LATENT + ROPE)
    keys = nd * groups * tile
    vmem = pl.BlockSpec(memory_space=pltpu.VMEM)
    hbm = pl.BlockSpec(memory_space=pl.ANY)
    smem = pl.BlockSpec(memory_space=pltpu.SMEM)
    bf, f32 = jnp.bfloat16, jnp.float32
    dma = pltpu.SemaphoreType.DMA
    return pl.pallas_call(
        functools.partial(kernel, blocks, groups, spacing, scale),
        out_shape=(
            jax.ShapeDtypeStruct(query_latent.shape, bf),
            jax.ShapeDtypeStruct(query_rotary.shape, bf),
            jax.ShapeDtypeStruct(latent.shape, f32),
            jax.ShapeDtypeStruct(key_rotary.shape, f32),
        ),
        in_specs=[hbm, hbm, hbm, vmem, vmem, smem],
        out_specs=(vmem, vmem, vmem, vmem),
        scratch_shapes=[
            pltpu.VMEM((rows, LATENT + 2 * ROPE), bf),
            pltpu.VMEM((rows, LATENT), bf),
            pltpu.VMEM(query_rotary.shape, bf),
            pltpu.VMEM((groups, nd, half, packed), bf),
            pltpu.VMEM((keys, LATENT + 2 * ROPE), bf),
            pltpu.VMEM((keys, rows), f32),
            pltpu.VMEM((keys, rows), f32),
            pltpu.VMEM((keys, rows), bf),
            pltpu.VMEM((keys, rows), bf),
            pltpu.VMEM((groups, nd, half, packed), bf),
            pltpu.VMEM((groups, half, packed), f32),
            pltpu.VMEM((groups, nd, half, packed), bf),
            pltpu.VMEM((groups, half, packed), bf),
            pltpu.VMEM((half, packed), f32),
            pltpu.VMEM((groups, half, packed), bf),
            dma((1 + 2 * heads,)),
            dma((groups,)),
            dma((groups,)),
            dma((groups, nd)),
            dma((groups, nd)),
            dma((groups, nd)),
            dma((groups, nd)),
            dma((groups,)),
            dma((groups,)),
        ],
        compiler_params=pltpu.CompilerParams(
            collective_id=0, has_side_effects=True, vmem_limit_bytes=50 * 1024 * 1024
        ),
        cost_estimate=pl.CostEstimate(flops=4_300_000_000, bytes_accessed=4_000_000, transcendentals=800_000),
    )(query_latent, query_rotary, upstream, latent, key_rotary, pattern)


def solution(mesh):
    in_specs = (
        P("blk", "inner"),
        P("blk", "inner"),
        P("blk", "inner"),
        P(("blk", "inner"), None),
        P(("blk", "inner"), None),
        P("blk", None),
    )
    out_specs = (
        P("blk", "inner"),
        P("blk", "inner"),
        P(("blk", "inner"), None),
        P(("blk", "inner"), None),
    )
    return jax.shard_map(
        per_device, mesh=mesh, in_specs=in_specs, out_specs=out_specs, check_vma=False
    )
```

time: 237 us -> 65.2 us (0.28)
  the two profiles are of different devices: /device:TPU:94 before, /device:TPU:9 now
where the time goes in v1:
time: 65.2 us; the launch traced here: 64.9 us
  Pallas kernels  55.9 us (86%)
  local copies, waits for them, and re-layouts  8.32 us (13%)
  between operations  0.66 us (1%)
    pallas_call x1, Pallas kernels, per_device(): pl.pallas_call(functools.partial(kernel, blocks, groups, spacing, scale),...  55.9 us
    unnamed x16, local copies, waits for them, and re-layouts  8.32 us

profile of v1, /device:TPU:9, one launch (start us, length us, event | category | flops | bytes accessed | tf_op | source)
XLA Modules:
  0.0 64.9 jit_solution(6194198432534920301)
XLA Ops:
  0.6 0.0 copy-start
  0.6 1.2 %copy-done = bf16[128,4096]{1,0:T(8,128)(2,1)S(1)} copy-done((bf16[128,4096]{1,0:T(8,128)(2,1)S(1)}, bf16[128,4096]{1,0:T(8,128)(2,1)}, u32[]{:S(2)}) %copy-start) | copy-done | bytes 1048600
  1.9 0.0 copy-start.1
  1.9 1.2 %copy-done.1 = bf16[128,4096]{1,0:T(8,128)(2,1)S(1)} copy-done((bf16[128,4096]{1,0:T(8,128)(2,1)S(1)}, bf16[128,4096]{1,0:T(8,128)(2,1)}, u32[]{:S(2)}) %copy-start.1) | copy-done | bytes 1048600
  3.1 0.0 copy-start.2
  3.1 0.9 %copy-done.2 = bf16[128,512]{1,0:T(8,128)(2,1)S(1)} copy-done((bf16[128,512]{1,0:T(8,128)(2,1)S(1)}, bf16[128,512]{1,0:T(8,128)(2,1)}, u32[]{:S(2)}) %copy-start.2) | copy-done | bytes 131096
  4.0 0.0 copy-start.3
  4.0 0.8 %copy-done.3 = bf16[32,512]{1,0:T(8,128)(2,1)S(1)} copy-done((bf16[32,512]{1,0:T(8,128)(2,1)S(1)}, bf16[32,512]{1,0:T(8,128)(2,1)}, u32[]{:S(2)}) %copy-start.3) | copy-done | bytes 32792
  4.7 0.0 copy-start.4
  4.7 0.7 %copy-done.4 = bf16[32,64]{1,0:T(8,128)(2,1)S(1)} copy-done((bf16[32,64]{1,0:T(8,128)(2,1)S(1)}, bf16[32,64]{1,0:T(8,128)(2,1)}, u32[]{:S(2)}) %copy-start.4) | copy-done | bytes 4120
  5.4 0.0 copy-start.5
  5.4 0.7 %copy-done.5 = s32[1,6]{1,0:T(1,128)S(1)} copy-done((s32[1,6]{1,0:T(1,128)S(1)}, s32[1,6]{1,0:T(1,128)}, u32[]{:S(2)}) %copy-start.5) | copy-done | bytes 48
  6.1 55.9 %shard_map.93 = (bf16[128,4096]{1,0:T(8,128)(2,1)S(1)}, bf16[128,512]{1,0:T(8,128)(2,1)S(1)}, f32[32,512]{1,0:T(8,128)S(1)}, f32[32,64]{1,0:T(8,128)S(1)}) custom-call(bf16[128,4096]{1,0:T(8,128)(2,1)S(1)} %copy-done, bf16[128,512]{1,0:T(8,128)(2,1)S(1)} %copy-done.2, bf16[128,4096]{1,0:T(8,128)(2,1)S(1)} %copy-done.1, bf16[32,512]{1,0:T(8,128)(2,1)S(1)} %copy-done.3, ...), custom_call_target="tpu_custom_call" | custom-call | flops 4300000256 | bytes 4000000 | tf_op jit(solution)/shard_map/pallas_call | solution.py:337
  62.0 1.0 %copy.14 = bf16[128,4096]{1,0:T(8,128)(2,1)} copy(bf16[128,4096]{1,0:T(8,128)(2,1)S(1)} %get-tuple-element.8) | data formatting | bytes 2097152
  63.0 0.7 %copy.15 = bf16[128,512]{1,0:T(8,128)(2,1)} copy(bf16[128,512]{1,0:T(8,128)(2,1)S(1)} %get-tuple-element.9) | data formatting | bytes 262144
  63.7 0.6 copy.16
  64.3 0.6 copy.17
Async XLA Ops:
  0.6 1.2 %copy-start = (bf16[128,4096]{1,0:T(8,128)(2,1)S(1)}, bf16[128,4096]{1,0:T(8,128)(2,1)}, u32[]{:S(2)}) copy-start(bf16[128,4096]{1,0:T(8,128)(2,1)} %q_hbm.1) | copy-start | bytes 3145732
  1.9 1.2 %copy-start.1 = (bf16[128,4096]{1,0:T(8,128)(2,1)S(1)}, bf16[128,4096]{1,0:T(8,128)(2,1)}, u32[]{:S(2)}) copy-start(bf16[128,4096]{1,0:T(8,128)(2,1)} %up_hbm.1) | copy-start | bytes 3145732
  3.1 0.9 %copy-start.2 = (bf16[128,512]{1,0:T(8,128)(2,1)S(1)}, bf16[128,512]{1,0:T(8,128)(2,1)}, u32[]{:S(2)}) copy-start(bf16[128,512]{1,0:T(8,128)(2,1)} %qr_hbm.1) | copy-start | bytes 393220
  4.0 0.8 %copy-start.3 = (bf16[32,512]{1,0:T(8,128)(2,1)S(1)}, bf16[32,512]{1,0:T(8,128)(2,1)}, u32[]{:S(2)}) copy-start(bf16[32,512]{1,0:T(8,128)(2,1)} %lat_ref.1) | copy-start | bytes 98308
  4.7 0.7 %copy-start.4 = (bf16[32,64]{1,0:T(8,128)(2,1)S(1)}, bf16[32,64]{1,0:T(8,128)(2,1)}, u32[]{:S(2)}) copy-start(bf16[32,64]{1,0:T(8,128)(2,1)} %kr_ref.1) | copy-start | bytes 12292
  5.4 0.7 %copy-start.5 = (s32[1,6]{1,0:T(1,128)S(1)}, s32[1,6]{1,0:T(1,128)}, u32[]{:S(2)}) copy-start(s32[1,6]{1,0:T(1,128)} %pat_ref.1) | copy-start | bytes 76

commit v2 on v1

v2 whole, which is shorter than its diff:
```python
import functools

import jax
import jax.numpy as jnp
from jax import lax
from jax.experimental import pallas as pl
from jax.experimental.pallas import tpu as pltpu
from jax.sharding import PartitionSpec as P

MESH = pl.DeviceIdType.MESH
LATENT = 512
ROPE = 64
NOPE = 128
WIN = 2
NSTR = 4
LOG2E = 1.4426950408889634
MASKED = -1e30
PLACE = {0: 0, 1: 1, 3: 2, 2: 3}
ARRIVALS = ((0,), (1, 3), (2,))
GRAD_ORDER = (2, 1, 3, 0)
RELAY_CUT = 640


def spacing_list(blocks):
    spacing = blocks // 8
    listed = set(range(WIN))
    for number in range(1, NSTR + 1):
        listed.add(number * spacing)
    return sorted(listed)


def kernel(
    blocks,
    groups,
    spacing,
    scale,
    q_hbm,
    qr_hbm,
    up_hbm,
    lat_hbm,
    kr_hbm,
    pat_hbm,
    qc_hbm,
    rc_ref,
    lc_ref,
    pc_ref,
    qcat,
    upcat,
    q_turned,
    up_turned,
    qrraw,
    lat_ref,
    kr_ref,
    pat_ref,
    kbuf,
    kcat,
    e_buf,
    dp_buf,
    ds_buf,
    w_buf,
    top_buf,
    sum_buf,
    mix_buf,
    qc_ref,
    gsend,
    gown,
    gbuf,
    rsend,
    rown,
    rbuf,
    small_sem,
    load_sem,
    out_sem,
    in_send,
    in_recv,
    k_send,
    k_recv,
    g_send,
    g_recv,
    r_send,
    r_recv,
):
    b = lax.axis_index("blk")
    i = lax.axis_index("inner")
    nd = len(spacing)
    heads = q_hbm.shape[1] // LATENT
    tokens = q_hbm.shape[0]
    rows = heads * tokens
    tile = lat_hbm.shape[0]
    half = tile // 2
    per_slot = nd * tile
    packed = kbuf.shape[3]
    bf = jnp.bfloat16
    f32 = jnp.float32

    def inner_peer(k):
        return (b, lax.rem(i + k, groups))

    def blk_peer(d):
        return (lax.rem(b + d + blocks, blocks), i)

    small = [
        pltpu.make_async_copy(lat_hbm, lat_ref, small_sem.at[0]),
        pltpu.make_async_copy(kr_hbm, kr_ref, small_sem.at[1]),
        pltpu.make_async_copy(pat_hbm, pat_ref, small_sem.at[2]),
    ]
    for load in small:
        load.start()

    barrier = pltpu.get_barrier_semaphore()
    partners = {d for d in spacing if d > 0} | {(-d) % blocks for d in spacing if d > 0}
    partners = sorted(partners)
    for k in (1, 3):
        pl.semaphore_signal(barrier, inc=1, device_id=inner_peer(k), device_id_type=MESH)
    for d in partners:
        pl.semaphore_signal(barrier, inc=1, device_id=blk_peer(d), device_id_type=MESH)

    qr_load = pltpu.make_async_copy(qr_hbm, qrraw, load_sem.at[0])
    qr_load.start()
    loads = []
    for h in range(heads):
        span = pl.ds(h * LATENT, LATENT)
        own = pl.ds(h * tokens, tokens)
        pair = (
            pltpu.make_async_copy(q_hbm.at[:, span], qcat.at[own, pl.ds(0, LATENT)], load_sem.at[1 + 2 * h]),
            pltpu.make_async_copy(up_hbm.at[:, span], upcat.at[own], load_sem.at[2 + 2 * h]),
        )
        for load in pair:
            load.start()
        loads.append(pair)

    for load in small:
        load.wait()
    kbuf[0, 0, :, 0:LATENT] = lat_ref[0:half]
    kbuf[0, 0, :, LATENT : 2 * LATENT] = lat_ref[half:tile]
    kbuf[0, 0, :, 2 * LATENT :] = jnp.concatenate([kr_ref[0:half], kr_ref[half:tile]], axis=1)

    pl.semaphore_wait(barrier, 2 + len(partners))

    sends = []

    def launch(copy):
        copy.start()
        sends.append(copy)

    def near_tile(k):
        back = groups - k
        return pltpu.make_async_remote_copy(
            src_ref=kbuf.at[0, 0],
            dst_ref=kbuf.at[back, 0],
            send_sem=in_send.at[k],
            recv_sem=in_recv.at[back],
            device_id=inner_peer(k),
            device_id_type=MESH,
        )

    def relayed_half(k, slot):
        span = pl.ds(0, RELAY_CUT) if k == 1 else pl.ds(RELAY_CUT, packed - RELAY_CUT)
        n = 0 if k == 1 else 2
        return pltpu.make_async_remote_copy(
            src_ref=kbuf.at[slot, 0, :, span],
            dst_ref=kbuf.at[2, 0, :, span],
            send_sem=in_send.at[n],
            recv_sem=in_recv.at[n],
            device_id=inner_peer(k),
            device_id_type=MESH,
        )

    def block_tile(k, n):
        return pltpu.make_async_remote_copy(
            src_ref=kbuf.at[k, 0],
            dst_ref=kbuf.at[k, n],
            send_sem=k_send.at[k, n],
            recv_sem=k_recv.at[k, n],
            device_id=blk_peer(spacing[n]),
            device_id_type=MESH,
        )

    def block_grad(k, n):
        return pltpu.make_async_remote_copy(
            src_ref=gsend.at[k, n],
            dst_ref=gbuf.at[k, n],
            send_sem=g_send.at[k, n],
            recv_sem=g_recv.at[k, n],
            device_id=blk_peer(-spacing[n]),
            device_id_type=MESH,
        )

    def inner_grad(k):
        back = groups - k
        return pltpu.make_async_remote_copy(
            src_ref=rsend.at[k],
            dst_ref=rbuf.at[back],
            send_sem=r_send.at[k],
            recv_sem=r_recv.at[back],
            device_id=inner_peer(k),
            device_id_type=MESH,
        )

    def forward(k):
        for n in (4, 5, 3, 2, 1):
            launch(block_tile(k, n))

    launch(near_tile(1))
    launch(near_tile(3))
    forward(0)

    qr_load.wait()
    lane = lax.broadcasted_iota(jnp.int32, (tokens, 2 * ROPE), 1)
    for h in range(heads):
        own = pl.ds(h * tokens, tokens)
        pair = qrraw[:, pl.ds((h // 2) * 2 * ROPE, 2 * ROPE)]
        keep = (lane < ROPE) if h % 2 == 0 else (lane >= ROPE)
        qcat[own, LATENT:] = jnp.where(keep, pair, jnp.zeros_like(pair))
        for load in loads[h]:
            load.wait()
        q_turned[:, own] = qcat[own, :].T
        up_turned[:, own] = upcat[own, :].T

    bias = [jnp.where(pat_ref[0, n] >= 0, 0.0, MASKED).astype(f32) for n in range(nd)]
    factor = scale * LOG2E
    lane_half = lax.broadcasted_iota(jnp.int32, (half, 2 * ROPE), 1)
    natural = (((1,), (0,)), ((), ()))

    def take_keys(k):
        for n in range(1, nd):
            block_tile(k, n).wait_recv()
        for n in range(nd):
            start = PLACE[k] * per_slot + n * tile
            kcat[pl.ds(start, half), 0:LATENT] = kbuf[k, n, :, 0:LATENT]
            kcat[pl.ds(start + half, half), 0:LATENT] = kbuf[k, n, :, LATENT : 2 * LATENT]
            both = kbuf[k, n, :, 2 * LATENT :].astype(f32)
            turned = pltpu.roll(both, ROPE, 1)
            kcat[pl.ds(start, half), LATENT:] = jnp.where(lane_half < ROPE, both, turned).astype(bf)
            kcat[pl.ds(start + half, half), LATENT:] = jnp.where(lane_half < ROPE, turned, both).astype(bf)

    def score(group):
        slots = ARRIVALS[group]
        base = PLACE[slots[0]] * per_slot
        count = len(slots) * per_slot
        span_rows = pl.ds(base, count)

        def step(p, carry):
            span = pl.ds(pl.multiple_of(p * 256, 256), 256)
            s = lax.dot_general(kcat[span_rows, :], q_turned[:, span], natural, preferred_element_type=f32) * factor
            dp = lax.dot_general(
                kcat[span_rows, 0:LATENT], up_turned[:, span], natural, preferred_element_type=f32
            )
            key_token = lax.broadcasted_iota(jnp.int32, (tile, 256), 0)
            row_token = lax.rem(lax.broadcasted_iota(jnp.int32, (tile, 256), 1), tokens)
            parts = []
            for m, k in enumerate(slots):
                for n in range(nd):
                    part = s[m * per_slot + n * tile : m * per_slot + (n + 1) * tile]
                    if n == 0:
                        first = lax.rem(i + k, groups) * tile
                        parts.append(jnp.where(key_token + first <= row_token, part, MASKED))
                    else:
                        parts.append(part + bias[n])
            s = jnp.concatenate(parts, axis=0)
            top = jnp.max(s, axis=0, keepdims=True)
            e = jnp.exp2(s - top)
            e_buf[span_rows, span] = e
            dp_buf[span_rows, span] = dp
            top_buf[group : group + 1, span] = top
            sum_buf[group : group + 1, span] = jnp.sum(e, axis=0, keepdims=True)
            mix_buf[group : group + 1, span] = jnp.sum(e * dp, axis=0, keepdims=True)
            return carry

        lax.fori_loop(0, rows // 256, step, 0)

    near_tile(1).wait_recv()
    launch(relayed_half(1, 3))
    near_tile(3).wait_recv()
    launch(relayed_half(3, 1))
    forward(3)
    forward(1)
    take_keys(0)
    score(0)
    relayed_half(1, 3).wait_recv()
    relayed_half(3, 1).wait_recv()
    forward(2)
    take_keys(1)
    take_keys(3)
    score(1)
    take_keys(2)
    score(2)

    tops = [top_buf[g : g + 1, :] for g in range(3)]
    top = jnp.maximum(jnp.maximum(tops[0], tops[1]), tops[2])
    fade = [jnp.exp2(t - top) for t in tops]
    total = sum(fade[g] * sum_buf[g : g + 1, :] for g in range(3))
    mix = sum(fade[g] * mix_buf[g : g + 1, :] for g in range(3))
    inverse = 1.0 / total
    mix_buf[3:4, :] = mix * inverse
    for g in range(3):
        sum_buf[4 + g : 5 + g, :] = fade[g] * inverse

    def pack_rows(g, n):
        lo = g[n * tile : n * tile + half]
        hi = g[n * tile + half : (n + 1) * tile]
        rlo = lo[:, LATENT:]
        rhi = hi[:, LATENT:]
        rlo = rlo + pltpu.roll(rlo, ROPE, 1)
        rhi = rhi + pltpu.roll(rhi, ROPE, 1)
        return lo[:, 0:LATENT], hi[:, 0:LATENT], jnp.where(lane_half < ROPE, rlo, rhi)

    for k in GRAD_ORDER:
        group = [g for g in range(3) if k in ARRIVALS[g]][0]
        span_rows = pl.ds(PLACE[k] * per_slot, per_slot)

        def weigh(p, carry, group=group, span_rows=span_rows):
            span = pl.ds(pl.multiple_of(p * 256, 256), 256)
            w = e_buf[span_rows, span] * sum_buf[4 + group : 5 + group, span]
            w_buf[span_rows, span] = w.astype(bf)
            ds_buf[span_rows, span] = (w * ((dp_buf[span_rows, span] - mix_buf[3:4, span]) * scale)).astype(bf)
            return carry

        lax.fori_loop(0, rows // 256, weigh, 0)
        dsk = ds_buf[span_rows, :]
        wk = w_buf[span_rows, :]
        g_lat = lax.dot_general(dsk, qcat[:, 0:LATENT], natural, preferred_element_type=f32)
        g_lat = g_lat + lax.dot_general(wk, upcat[...], natural, preferred_element_type=f32)
        g_rot = lax.dot_general(dsk, qcat[:, LATENT:], natural, preferred_element_type=f32)
        g = jnp.concatenate([g_lat, g_rot], axis=1)
        for n in range(nd):
            lo, hi, rot = pack_rows(g, n)
            if n == 0:
                gown[k, :, 0:LATENT] = lo
                gown[k, :, LATENT : 2 * LATENT] = hi
                gown[k, :, 2 * LATENT :] = rot
            else:
                gsend[k, n, :, 0:LATENT] = lo.astype(bf)
                gsend[k, n, :, LATENT : 2 * LATENT] = hi.astype(bf)
                gsend[k, n, :, 2 * LATENT :] = rot.astype(bf)
        for n in (4, 5, 3, 2, 1):
            launch(block_grad(k, n))

    outs = []
    lane_tok = lax.broadcasted_iota(jnp.int32, (tokens, 2 * ROPE), 1)
    for p in range(heads // 2):
        turned = []
        for h in (2 * p, 2 * p + 1):
            span = pl.ds(h * tokens, tokens)
            dq = lax.dot_general(ds_buf[:, span], kcat[...], (((0,), (0,)), ((), ())), preferred_element_type=f32)
            qc_ref[:, pl.ds(h * LATENT, LATENT)] = dq[:, 0:LATENT].astype(bf)
            turned.append(dq[:, LATENT:])
        rc_ref[:, pl.ds(p * 2 * ROPE, 2 * ROPE)] = jnp.where(lane_tok < ROPE, turned[0], turned[1]).astype(bf)
    out = pltpu.make_async_copy(qc_ref, qc_hbm, out_sem.at[0])
    out.start()

    for k in GRAD_ORDER:
        total = gown[k]
        for n in range(1, nd):
            block_grad(k, n).wait_recv()
            total = total + gbuf[k, n].astype(f32)
        if k == 0:
            rown[...] = total
        else:
            rsend[k] = total.astype(bf)
            launch(inner_grad(k))

    total = rown[...]
    for k in range(1, groups):
        inner_grad(groups - k).wait_recv()
        total = total + rbuf[k].astype(f32)
    lc_ref[0:half, :] = total[:, 0:LATENT]
    lc_ref[half:tile, :] = total[:, LATENT : 2 * LATENT]
    pc_ref[0:half, :] = total[:, 2 * LATENT : 2 * LATENT + ROPE]
    pc_ref[half:tile, :] = total[:, 2 * LATENT + ROPE :]
    for copy in sends:
        copy.wait_send()
    out.wait()


def place_results(qc_in, rc_in, lc_in, pc_in, qc_out, rc_out, lc_out, pc_out, qc_buf, rc_buf, lc_buf, pc_buf, sems):
    strip = 16
    moves = []
    for r in range(0, qc_in.shape[0], strip):
        rows = pl.ds(r, strip)
        moves.append((qc_in.at[rows], qc_buf.at[rows], qc_out.at[rows]))
    moves += [(rc_in, rc_buf, rc_out), (lc_in, lc_buf, lc_out), (pc_in, pc_buf, pc_out)]
    steps = [
        (pltpu.make_async_copy(src, mid, sems.at[0, n]), pltpu.make_async_copy(mid, dst, sems.at[1, n]))
        for n, (src, mid, dst) in enumerate(moves)
    ]
    for load, _ in steps:
        load.start()
    for load, store in steps:
        load.wait()
        store.start()
    for _, store in steps:
        store.wait()


def per_device(query_latent, query_rotary, upstream, latent, key_rotary, pattern):
    blocks = lax.axis_size("blk")
    groups = lax.axis_size("inner")
    spacing = spacing_list(blocks)
    nd = len(spacing)
    scale = (NOPE + ROPE) ** (-0.5)
    tokens, width = query_latent.shape
    heads = width // LATENT
    rows = heads * tokens
    tile = latent.shape[0]
    half = tile // 2
    packed = 2 * (LATENT + ROPE)
    keys = nd * groups * tile
    vmem = pl.BlockSpec(memory_space=pltpu.VMEM)
    hbm = pl.BlockSpec(memory_space=pltpu.HBM)
    bf, f32 = jnp.bfloat16, jnp.float32
    dma = pltpu.SemaphoreType.DMA
    outs = pl.pallas_call(
        functools.partial(kernel, blocks, groups, spacing, scale),
        out_shape=(
            jax.ShapeDtypeStruct(query_latent.shape, bf),
            jax.ShapeDtypeStruct(query_rotary.shape, bf),
            jax.ShapeDtypeStruct(latent.shape, f32),
            jax.ShapeDtypeStruct(key_rotary.shape, f32),
        ),
        in_specs=[hbm] * 6,
        out_specs=(hbm, vmem, vmem, vmem),
        scratch_shapes=[
            pltpu.VMEM((rows, LATENT + 2 * ROPE), bf),
            pltpu.VMEM((rows, LATENT), bf),
            pltpu.VMEM((LATENT + 2 * ROPE, rows), bf),
            pltpu.VMEM((LATENT, rows), bf),
            pltpu.VMEM(query_rotary.shape, bf),
            pltpu.VMEM(latent.shape, bf),
            pltpu.VMEM(key_rotary.shape, bf),
            pltpu.SMEM(pattern.shape, jnp.int32),
            pltpu.VMEM((groups, nd, half, packed), bf),
            pltpu.VMEM((keys, LATENT + 2 * ROPE), bf),
            pltpu.VMEM((keys, rows), f32),
            pltpu.VMEM((keys, rows), f32),
            pltpu.VMEM((keys, rows), bf),
            pltpu.VMEM((keys, rows), bf),
            pltpu.VMEM((8, rows), f32),
            pltpu.VMEM((8, rows), f32),
            pltpu.VMEM((8, rows), f32),
            pltpu.VMEM(query_latent.shape, bf),
            pltpu.VMEM((groups, nd, half, packed), bf),
            pltpu.VMEM((groups, half, packed), f32),
            pltpu.VMEM((groups, nd, half, packed), bf),
            pltpu.VMEM((groups, half, packed), bf),
            pltpu.VMEM((half, packed), f32),
            pltpu.VMEM((groups, half, packed), bf),
            dma((3,)),
            dma((1 + 2 * heads,)),
            dma((1,)),
            dma((groups,)),
            dma((groups,)),
            dma((groups, nd)),
            dma((groups, nd)),
            dma((groups, nd)),
            dma((groups, nd)),
            dma((groups,)),
            dma((groups,)),
        ],
        compiler_params=pltpu.CompilerParams(
            collective_id=0, has_side_effects=True, vmem_limit_bytes=60 * 1024 * 1024
        ),
        cost_estimate=pl.CostEstimate(flops=4_300_000_000, bytes_accessed=4_000_000, transcendentals=800_000),
    )(query_latent, query_rotary, upstream, latent, key_rotary, pattern)
    return pl.pallas_call(
        place_results,
        out_shape=tuple(jax.ShapeDtypeStruct(x.shape, x.dtype) for x in outs),
        in_specs=[hbm] * 4,
        out_specs=tuple([hbm] * 4),
        scratch_shapes=[pltpu.VMEM(x.shape, x.dtype) for x in outs] + [dma((2, tokens // 16 + 3))],
        compiler_params=pltpu.CompilerParams(vmem_limit_bytes=60 * 1024 * 1024),
    )(*outs)


def solution(mesh):
    in_specs = (
        P("blk", "inner"),
        P("blk", "inner"),
        P("blk", "inner"),
        P(("blk", "inner"), None),
        P(("blk", "inner"), None),
        P("blk", None),
    )
    out_specs = (
        P("blk", "inner"),
        P("blk", "inner"),
        P(("blk", "inner"), None),
        P(("blk", "inner"), None),
    )
    return jax.shard_map(
        per_device, mesh=mesh, in_specs=in_specs, out_specs=out_specs, check_vma=False
    )
```

time: 65.2 us -> 54.7 us (0.84)
  the two profiles are of different devices: /device:TPU:9 before, /device:TPU:4 now
where the time goes in v2:
time: 54.7 us; the launch traced here: 54.5 us
  Pallas kernels  53.9 us (99%)
  between operations  0.64 us (1%)
    pallas_call x1, Pallas kernels, per_device(): pl.pallas_call(functools.partial(kernel, blocks, groups, spacing, scale),...  51.7 us
    pallas_call x1, Pallas kernels, per_device(): pl.pallas_call(place_results, out_shape=tuple((jax.ShapeDtypeStruct(x.sha...  2.2 us

profile of v2, /device:TPU:4, one launch (start us, length us, event | category | flops | bytes accessed | tf_op | source)
XLA Modules:
  0.0 54.5 jit_solution(5703429349737411152)
XLA Ops:
  0.6 51.7 %shard_map.93 = (bf16[128,4096]{1,0:T(8,128)(2,1)}, bf16[128,512]{1,0:T(8,128)(2,1)}, f32[32,512]{1,0:T(8,128)}, f32[32,64]{1,0:T(8,128)}) custom-call(bf16[128,4096]{1,0:T(8,128)(2,1)} %q_hbm.1, bf16[128,512]{1,0:T(8,128)(2,1)} %qr_hbm.1, bf16[128,4096]{1,0:T(8,128)(2,1)} %up_hbm.1, bf16[32,512]{1,0:T(8,128)(2,1)} %lat_hbm.1, bf16[32,64]{1,0:T(8,128)(2,1)} %kr_hbm.1, ...), custom_call_target="tpu_custom_call" | custom-call | flops 4300000256 | bytes 4000000 | tf_op jit(solution)/shard_map/pallas_call | solution.py:413
  52.3 2.2 %shard_map.94 = (bf16[128,4096]{1,0:T(8,128)(2,1)}, bf16[128,512]{1,0:T(8,128)(2,1)}, f32[32,512]{1,0:T(8,128)}, f32[32,64]{1,0:T(8,128)}) custom-call(bf16[128,4096]{1,0:T(8,128)(2,1)} %get-tuple-element.8.qc_in, bf16[128,512]{1,0:T(8,128)(2,1)} %get-tuple-element.9.rc_in, f32[32,512]{1,0:T(8,128)} %get-tuple-element.10.lc_in, f32[32,64]{1,0:T(8,128)} %get-tuple-element.11.pc_in), custom_call_target="tpu_custom_call" | custom-call | tf_op jit(solution)/shard_map/pallas_call | solution.py:465

commit v3 on v2

--- a/solution.py
+++ b/solution.py
@@ -17,7 +17,6 @@
 MASKED = -1e30
 PLACE = {0: 0, 1: 1, 3: 2, 2: 3}
 ARRIVALS = ((0,), (1, 3), (2,))
-GRAD_ORDER = (2, 1, 3, 0)
 RELAY_CUT = 640
 
 
@@ -40,7 +39,7 @@
     lat_hbm,
     kr_hbm,
     pat_hbm,
-    qc_hbm,
+    qc_ref,
     rc_ref,
     lc_ref,
     pc_ref,
@@ -61,7 +60,7 @@
     top_buf,
     sum_buf,
     mix_buf,
-    qc_ref,
+    norm_buf,
     gsend,
     gown,
     gbuf,
@@ -70,7 +69,6 @@
     rbuf,
     small_sem,
     load_sem,
-    out_sem,
     in_send,
     in_recv,
     k_send,
@@ -104,9 +102,6 @@
         pltpu.make_async_copy(kr_hbm, kr_ref, small_sem.at[1]),
         pltpu.make_async_copy(pat_hbm, pat_ref, small_sem.at[2]),
     ]
-    for load in small:
-        load.start()
-
     barrier = pltpu.get_barrier_semaphore()
     partners = {d for d in spacing if d > 0} | {(-d) % blocks for d in spacing if d > 0}
     partners = sorted(partners)
@@ -115,6 +110,8 @@
     for d in partners:
         pl.semaphore_signal(barrier, inc=1, device_id=blk_peer(d), device_id_type=MESH)
 
+    for load in small:
+        load.start()
     qr_load = pltpu.make_async_copy(qr_hbm, qrraw, load_sem.at[0])
     qr_load.start()
     loads = []
@@ -143,28 +140,21 @@
         copy.start()
         sends.append(copy)
 
-    def near_tile(k):
-        back = groups - k
+    spans = (pl.ds(0, RELAY_CUT), pl.ds(RELAY_CUT, packed - RELAY_CUT))
+
+    def inner_half(n, k, part, source, target):
         return pltpu.make_async_remote_copy(
-            src_ref=kbuf.at[0, 0],
-            dst_ref=kbuf.at[back, 0],
-            send_sem=in_send.at[k],
-            recv_sem=in_recv.at[back],
-            device_id=inner_peer(k),
-            device_id_type=MESH,
-        )
-
-    def relayed_half(k, slot):
-        span = pl.ds(0, RELAY_CUT) if k == 1 else pl.ds(RELAY_CUT, packed - RELAY_CUT)
-        n = 0 if k == 1 else 2
-        return pltpu.make_async_remote_copy(
-            src_ref=kbuf.at[slot, 0, :, span],
-            dst_ref=kbuf.at[2, 0, :, span],
+            src_ref=kbuf.at[source, 0, :, spans[part]],
+            dst_ref=kbuf.at[target, 0, :, spans[part]],
             send_sem=in_send.at[n],
             recv_sem=in_recv.at[n],
             device_id=inner_peer(k),
             device_id_type=MESH,
         )
+
+    near_first = (inner_half(0, 1, 0, 0, 3), inner_half(1, 3, 1, 0, 1))
+    near_second = (inner_half(2, 1, 1, 0, 3), inner_half(3, 3, 0, 0, 1))
+    relayed = (inner_half(4, 1, 0, 3, 2), inner_half(5, 3, 1, 1, 2))
 
     def block_tile(k, n):
         return pltpu.make_async_remote_copy(
@@ -187,7 +177,7 @@
         )
 
     def inner_grad(k):
-        back = groups - k
+        back = lax.rem(groups - k, groups)
         return pltpu.make_async_remote_copy(
             src_ref=rsend.at[k],
             dst_ref=rbuf.at[back],
@@ -201,8 +191,8 @@
         for n in (4, 5, 3, 2, 1):
             launch(block_tile(k, n))
 
-    launch(near_tile(1))
-    launch(near_tile(3))
+    for copy in near_first + near_second:
+        launch(copy)
     forward(0)
 
     qr_load.wait()
@@ -267,18 +257,18 @@
             mix_buf[group : group + 1, span] = jnp.sum(e * dp, axis=0, keepdims=True)
             return carry
 
-        lax.fori_loop(0, rows // 256, step, 0)
-
-    near_tile(1).wait_recv()
-    launch(relayed_half(1, 3))
-    near_tile(3).wait_recv()
-    launch(relayed_half(3, 1))
-    forward(3)
-    forward(1)
+        lax.fori_loop(0, rows // 256, step, 0, unroll=True)
+
+    for n in range(2):
+        near_first[n].wait_recv()
+        launch(relayed[n])
+    for n in range(2):
+        near_second[n].wait_recv()
+        forward(3 - 2 * n)
     take_keys(0)
     score(0)
-    relayed_half(1, 3).wait_recv()
-    relayed_half(3, 1).wait_recv()
+    for copy in relayed:
+        copy.wait_recv()
     forward(2)
     take_keys(1)
     take_keys(3)
@@ -293,8 +283,8 @@
     mix = sum(fade[g] * mix_buf[g : g + 1, :] for g in range(3))
     inverse = 1.0 / total
     mix_buf[3:4, :] = mix * inverse
-    for g in range(3):
-        sum_buf[4 + g : 5 + g, :] = fade[g] * inverse
+    for p in range(groups):
+        norm_buf[p, 0:1, :] = fade[(p + 1) // 2] * inverse
 
     def pack_rows(g, n):
         lo = g[n * tile : n * tile + half]
@@ -305,25 +295,26 @@
         rhi = rhi + pltpu.roll(rhi, ROPE, 1)
         return lo[:, 0:LATENT], hi[:, 0:LATENT], jnp.where(lane_half < ROPE, rlo, rhi)
 
-    for k in GRAD_ORDER:
-        group = [g for g in range(3) if k in ARRIVALS[g]][0]
-        span_rows = pl.ds(PLACE[k] * per_slot, per_slot)
-
-        def weigh(p, carry, group=group, span_rows=span_rows):
+    for target in range(groups):
+        k = lax.rem(target - i + groups, groups)
+        place = k + (k // 2) * (5 - 2 * k)
+        span_rows = pl.ds(pl.multiple_of(place * per_slot, per_slot), per_slot)
+
+        def weigh(p, carry, place=place, span_rows=span_rows):
             span = pl.ds(pl.multiple_of(p * 256, 256), 256)
-            w = e_buf[span_rows, span] * sum_buf[4 + group : 5 + group, span]
+            w = e_buf[span_rows, span] * norm_buf[place, 0:1, span]
             w_buf[span_rows, span] = w.astype(bf)
             ds_buf[span_rows, span] = (w * ((dp_buf[span_rows, span] - mix_buf[3:4, span]) * scale)).astype(bf)
             return carry
 
-        lax.fori_loop(0, rows // 256, weigh, 0)
+        lax.fori_loop(0, rows // 256, weigh, 0, unroll=True)
         dsk = ds_buf[span_rows, :]
         wk = w_buf[span_rows, :]
         g_lat = lax.dot_general(dsk, qcat[:, 0:LATENT], natural, preferred_element_type=f32)
         g_lat = g_lat + lax.dot_general(wk, upcat[...], natural, preferred_element_type=f32)
         g_rot = lax.dot_general(dsk, qcat[:, LATENT:], natural, preferred_element_type=f32)
         g = jnp.concatenate([g_lat, g_rot], axis=1)
-        for n in range(nd):
+        for n in (5, 4, 3, 2, 1, 0):
             lo, hi, rot = pack_rows(g, n)
             if n == 0:
                 gown[k, :, 0:LATENT] = lo
@@ -333,8 +324,7 @@
                 gsend[k, n, :, 0:LATENT] = lo.astype(bf)
                 gsend[k, n, :, LATENT : 2 * LATENT] = hi.astype(bf)
                 gsend[k, n, :, 2 * LATENT :] = rot.astype(bf)
-        for n in (4, 5, 3, 2, 1):
-            launch(block_grad(k, n))
+                launch(block_grad(k, n))
 
     outs = []
     lane_tok = lax.broadcasted_iota(jnp.int32, (tokens, 2 * ROPE), 1)
@@ -346,19 +336,22 @@
             qc_ref[:, pl.ds(h * LATENT, LATENT)] = dq[:, 0:LATENT].astype(bf)
             turned.append(dq[:, LATENT:])
         rc_ref[:, pl.ds(p * 2 * ROPE, 2 * ROPE)] = jnp.where(lane_tok < ROPE, turned[0], turned[1]).astype(bf)
-    out = pltpu.make_async_copy(qc_ref, qc_hbm, out_sem.at[0])
-    out.start()
-
-    for k in GRAD_ORDER:
+
+    for target in range(groups):
+        k = lax.rem(target - i + groups, groups)
         total = gown[k]
         for n in range(1, nd):
             block_grad(k, n).wait_recv()
             total = total + gbuf[k, n].astype(f32)
-        if k == 0:
+
+        @pl.when(target == i)
+        def _(total=total):
             rown[...] = total
-        else:
+
+        @pl.when(target != i)
+        def _(total=total, k=k):
             rsend[k] = total.astype(bf)
-            launch(inner_grad(k))
+            inner_grad(k).start()
 
     total = rown[...]
     for k in range(1, groups):
@@ -370,27 +363,16 @@
     pc_ref[half:tile, :] = total[:, 2 * LATENT + ROPE :]
     for copy in sends:
         copy.wait_send()
-    out.wait()
-
-
-def place_results(qc_in, rc_in, lc_in, pc_in, qc_out, rc_out, lc_out, pc_out, qc_buf, rc_buf, lc_buf, pc_buf, sems):
-    strip = 16
-    moves = []
-    for r in range(0, qc_in.shape[0], strip):
-        rows = pl.ds(r, strip)
-        moves.append((qc_in.at[rows], qc_buf.at[rows], qc_out.at[rows]))
-    moves += [(rc_in, rc_buf, rc_out), (lc_in, lc_buf, lc_out), (pc_in, pc_buf, pc_out)]
-    steps = [
-        (pltpu.make_async_copy(src, mid, sems.at[0, n]), pltpu.make_async_copy(mid, dst, sems.at[1, n]))
-        for n, (src, mid, dst) in enumerate(moves)
-    ]
-    for load, _ in steps:
-        load.start()
-    for load, store in steps:
-        load.wait()
-        store.start()
-    for _, store in steps:
-        store.wait()
+    for k in range(1, groups):
+        inner_grad(k).wait_send()
+
+
+def place_results(*refs):
+    copies = [pltpu.make_async_copy(refs[n], refs[4 + n], refs[8].at[n]) for n in range(4)]
+    for copy in copies:
+        copy.start()
+    for copy in copies:
+        copy.wait()
 
 
 def per_device(query_latent, query_rotary, upstream, latent, key_rotary, pattern):
@@ -413,13 +395,13 @@
     outs = pl.pallas_call(
         functools.partial(kernel, blocks, groups, spacing, scale),
         out_shape=(
-            jax.ShapeDtypeStruct(query_latent.shape, bf),
-            jax.ShapeDtypeStruct(query_rotary.shape, bf),
-            jax.ShapeDtypeStruct(latent.shape, f32),
-            jax.ShapeDtypeStruct(key_rotary.shape, f32),
+            pltpu.VMEM(query_latent.shape, bf),
+            pltpu.VMEM(query_rotary.shape, bf),
+            pltpu.VMEM(latent.shape, f32),
+            pltpu.VMEM(key_rotary.shape, f32),
         ),
         in_specs=[hbm] * 6,
-        out_specs=(hbm, vmem, vmem, vmem),
+        out_specs=(vmem, vmem, vmem, vmem),
         scratch_shapes=[
             pltpu.VMEM((rows, LATENT + 2 * ROPE), bf),
             pltpu.VMEM((rows, LATENT), bf),
@@ -438,7 +420,7 @@
             pltpu.VMEM((8, rows), f32),
             pltpu.VMEM((8, rows), f32),
             pltpu.VMEM((8, rows), f32),
-            pltpu.VMEM(query_latent.shape, bf),
+            pltpu.VMEM((groups, 8, rows), f32),
             pltpu.VMEM((groups, nd, half, packed), bf),
             pltpu.VMEM((groups, half, packed), f32),
             pltpu.VMEM((groups, nd, half, packed), bf),
@@ -447,9 +429,8 @@
             pltpu.VMEM((groups, half, packed), bf),
             dma((3,)),
             dma((1 + 2 * heads,)),
-            dma((1,)),
-            dma((groups,)),
-            dma((groups,)),
+            dma((6,)),
+            dma((6,)),
             dma((groups, nd)),
             dma((groups, nd)),
             dma((groups, nd)),
@@ -465,10 +446,10 @@
     return pl.pallas_call(
         place_results,
         out_shape=tuple(jax.ShapeDtypeStruct(x.shape, x.dtype) for x in outs),
-        in_specs=[hbm] * 4,
+        in_specs=[vmem] * 4,
         out_specs=tuple([hbm] * 4),
-        scratch_shapes=[pltpu.VMEM(x.shape, x.dtype) for x in outs] + [dma((2, tokens // 16 + 3))],
-        compiler_params=pltpu.CompilerParams(vmem_limit_bytes=60 * 1024 * 1024),
+        scratch_shapes=[dma((4,))],
+        compiler_params=pltpu.CompilerParams(vmem_limit_bytes=1024 * 1024),
     )(*outs)
 
 

time: 54.7 us -> 50.8 us (0.929)
  Pallas kernels: 53.9 us -> 50 us
    pallas_call x1, Pallas kernels: 51.7 us -> 49 us  [per_device(): pl.pallas_call(functools.partial(kernel, blocks, groups, spacing, scale),...]
    pallas_call x1, Pallas kernels: 2.2 us -> 1.06 us  [per_device(): pl.pallas_call(place_results, out_shape=tuple((jax.ShapeDtypeStruct(x.sha...]
where the time goes in v3:
time: 50.8 us; the launch traced here: 50.7 us
  Pallas kernels  50 us (98%)
  between operations  0.64 us (1%)
    pallas_call x1, Pallas kernels, per_device(): pl.pallas_call(functools.partial(kernel, blocks, groups, spacing, scale),...  49 us
    pallas_call x1, Pallas kernels, per_device(): pl.pallas_call(place_results, out_shape=tuple((jax.ShapeDtypeStruct(x.sha...  1.06 us

profile of v3, /device:TPU:4, one launch (start us, length us, event | category | flops | bytes accessed | tf_op | source)
XLA Modules:
  0.0 50.7 jit_solution(1751379284853107944)
XLA Ops:
  0.6 49.0 %shard_map.93 = (bf16[128,4096]{1,0:T(8,128)(2,1)S(1)}, bf16[128,512]{1,0:T(8,128)(2,1)S(1)}, f32[32,512]{1,0:T(8,128)S(1)}, f32[32,64]{1,0:T(8,128)S(1)}) custom-call(bf16[128,4096]{1,0:T(8,128)(2,1)} %q_hbm.1, bf16[128,512]{1,0:T(8,128)(2,1)} %qr_hbm.1, bf16[128,4096]{1,0:T(8,128)(2,1)} %up_hbm.1, bf16[32,512]{1,0:T(8,128)(2,1)} %lat_hbm.1, ...), custom_call_target="tpu_custom_call" | custom-call | flops 4300000256 | bytes 4000000 | tf_op jit(solution)/shard_map/pallas_call | solution.py:395
  49.6 1.1 %shard_map.94 = (bf16[128,4096]{1,0:T(8,128)(2,1)}, bf16[128,512]{1,0:T(8,128)(2,1)}, f32[32,512]{1,0:T(8,128)}, f32[32,64]{1,0:T(8,128)}) custom-call(bf16[128,4096]{1,0:T(8,128)(2,1)S(1)} %get-tuple-element.8.refs_0_, bf16[128,512]{1,0:T(8,128)(2,1)S(1)} %get-tuple-element.9.refs_1_, f32[32,512]{1,0:T(8,128)S(1)} %get-tuple-element.10.refs_2_, ...), custom_call_target="tpu_custom_call" | custom-call | tf_op jit(solution)/shard_map/pallas_call | solution.py:446
